TPU v7x, 512 devices: a whole 4x4x16 slice. The times are simulated.
512 devices in a mesh: kg: 16 (over z_hi, y, core), pt: 32 (over x, z_lo).
Axes of the slice: x: 4, y: 4, z: 16 (z_hi: 2, z_lo: 8; z = z_hi * 8 + z_lo), core: 2. Of those that a mesh axis runs over, the one named last changes fastest.
Arguments:
- left_orbitals: bfloat16 [2, 64, 4096, 512], P(None, 'kg', 'pt'), may hold values from -6 to 6
- right_orbitals: bfloat16 [2, 64, 512, 512], P(None, 'kg', 'pt'), may hold values from -0.25 to 0.25
- coulomb: bfloat16 [64, 512, 4096], P(None, 'kg', 'pt'), may hold values from 0.049804688 to 0.5
Outputs:
- exchange_applied: float32 [2, 64, 4096, 512], P(None, 'kg', 'pt')
All inputs are finite; a program needn't handle non-finite values.
Results may differ from a plain program's by a relative error of at most 0.0038.
Values may be sent and summed in bfloat16 or wider, within the bound.
No kernel may reach another device: no remote copies, remote signals or barrier semaphores. Data moves between devices by JAX's collectives and lax.ppermute only.
A program may use at most 64 MiB of HBM per device.

v0:
```python
import jax
import jax.numpy as jnp
from jax import lax
from jax.sharding import PartitionSpec as P


def dft_tables(count):
    index = jnp.arange(count, dtype=jnp.int32)
    digit_one = index // 16
    digit_two = index // 4 % 4
    digit_three = index % 4
    phase = (
        digit_one[:, None] * digit_one[None, :]
        + digit_two[:, None] * digit_two[None, :]
        + digit_three[:, None] * digit_three[None, :]
    ) % 4
    cos_table = jnp.where(phase == 0, 1.0, jnp.where(phase == 2, -1.0, 0.0)).astype(jnp.float32)
    sin_table = jnp.where(phase == 1, 1.0, jnp.where(phase == 3, -1.0, 0.0)).astype(jnp.float32)
    return (cos_table, sin_table)


def cross(first, second):
    return jnp.einsum("kni,kmi->knm", first, second, preferred_element_type=jnp.float32)


def apply(first, second):
    return jnp.einsum("knm,kni->kmi", first, second, preferred_element_type=jnp.float32)


def kernel_terms(kernel, piece):
    out_re = apply(kernel[0], piece[0]) - apply(kernel[1], piece[1])
    out_im = apply(kernel[0], piece[1]) + apply(kernel[1], piece[0])
    return jnp.stack([out_re, out_im])


def spectral(columns, coulomb):
    shape = columns.shape
    count = shape[1]
    cos_table, sin_table = dft_tables(count)
    forward = jnp.concatenate(
        [jnp.concatenate([cos_table, sin_table], 1), jnp.concatenate([-sin_table, cos_table], 1)], 0
    ).astype(jnp.bfloat16)
    backward = jnp.concatenate(
        [jnp.concatenate([cos_table, -sin_table], 1), jnp.concatenate([sin_table, cos_table], 1)], 0
    ).astype(jnp.bfloat16)
    freq = jnp.dot(
        forward, columns.reshape(2 * count, -1), preferred_element_type=jnp.float32
    ).reshape(shape)
    weighted = (coulomb[None].astype(jnp.float32) * freq).astype(jnp.bfloat16)
    spatial = jnp.dot(
        backward, weighted.reshape(2 * count, -1), preferred_element_type=jnp.float32
    ) * (1.0 / count)
    return spatial.astype(jnp.bfloat16).reshape(shape)


def on_device(left_orbitals, right_orbitals, coulomb):
    left_re = left_orbitals[0]
    left_im = left_orbitals[1]
    piece = lax.all_gather(right_orbitals, "pt", axis=2, tiled=True)
    pair_re = cross(piece[0], left_re) + cross(piece[1], left_im)
    pair_im = cross(piece[0], left_im) - cross(piece[1], left_re)
    pairs = jnp.stack([pair_re, pair_im]).astype(jnp.bfloat16)
    columns = lax.all_to_all(pairs, "kg", split_axis=2, concat_axis=1, tiled=True)
    spatial = spectral(columns, coulomb)
    kernel = lax.all_to_all(spatial, "kg", split_axis=1, concat_axis=2, tiled=True)
    return kernel_terms(kernel, lax.all_gather(right_orbitals, "pt", axis=2, tiled=True))


def solution(mesh):
    in_specs = (P(None, "kg", "pt", None), P(None, "kg", "pt", None), P(None, "kg", "pt"))
    out_specs = P(None, "kg", "pt", None)
    return jax.shard_map(
        on_device, mesh=mesh, in_specs=in_specs, out_specs=out_specs, check_vma=False
    )
```

profile of v0, /device:TPU:39, one launch (start us, length us, event | category | flops | bytes accessed | tf_op | source)
XLA Modules:
  0.0 376.8 jit_solution(10838197598014243151)
XLA Ops:
  6.5 0.7 all-gather.2.cloned.1.call-update
  7.3 203.8 %all-gather.2.cloned.1.call-done = bf16[2,4,512,512]{3,2,1,0:T(8,128)(2,1)} async-done(((bf16[2,4,16,512]{3,2,1,0:T(8,128)(2,1)}), bf16[2,4,512,512]{3,2,1,0:T(8,128)(2,1)}) %all-gather.2.cloned.1.call-update) | async-done | bytes 4194320 | tf_op jit(solution)/shard_map/all_gather | solution.py:59
  211.0 2.5 fusion.5
  213.5 0.4 copy-done
  214.0 1.8 fusion.6
  215.8 0.7 fusion.10
  216.6 0.7 fusion.11
  217.3 0.1 pad_maximum_fusion.1
  217.4 0.0 copy-start.2
  217.4 1.8 copy.25
  219.2 31.8 %all-to-all-start = ((bf16[2,4,512,128]{3,1,0,2:T(4,128)(2,1)}), bf16[2,4,512,128]{3,1,0,2:T(4,128)(2,1)S(1)}, u32[]{:S(2)}, u32[]{:S(2)}) async-start(bf16[2,4,512,128]{3,1,0,2:T(4,128)(2,1)} %copy.25), calls=%async_computation | async-start | bytes 2097152 | tf_op jit(solution)/shard_map/all_to_all | solution.py:63
  251.0 0.2 copy.24
  251.2 0.1 fusion.28
  251.3 0.1 fusion.24
  251.4 35.3 %all-to-all-done = bf16[2,4,512,128]{3,1,0,2:T(4,128)(2,1)S(1)} async-done(((bf16[2,4,512,128]{3,1,0,2:T(4,128)(2,1)}), bf16[2,4,512,128]{3,1,0,2:T(4,128)(2,1)S(1)}, u32[]{:S(2)}, u32[]{:S(2)}) %all-to-all-start) | async-done | bytes 1048608 | tf_op jit(solution)/shard_map/all_to_all | solution.py:63
  286.8 0.3 copy.26
  287.0 0.5 copy.50
  287.5 0.7 copy.27
  288.1 0.4 multiply_convert_fusion
  288.6 0.7 copy.28
  289.3 0.5 fusion.1
  289.8 0.2 copy.44
  290.1 0.1 copy.29
  290.2 73.9 %all_to_all.30 = bf16[2,64,32,128]{3,2,0,1:T(8,128)(2,1)S(1)} all-to-all(bf16[2,64,32,128]{3,2,0,1:T(8,128)(2,1)S(1)} %copy.29), channel_id=1, replica_groups=mesh['kg'=16,'pt'=32] {'kg'}, dimensions={1} | all-to-all | bytes 2097152 | tf_op jit(solution)/shard_map/all_to_all | solution.py:65
  364.1 0.1 copy.30
  364.2 0.1 fusion.31
  364.4 2.0 copy-done.1
  366.4 0.5 fusion.7
  366.9 0.5 fusion.4
  367.4 0.5 fusion.2
  367.9 0.5 fusion.3
  368.4 1.6 pad_maximum_fusion
  (10 shorter events, 0.1 us)
Async XLA Ops:
  6.5 204.5 %all-gather.2.cloned.1.call-start = ((), (), s32[]{:S(2)}) async-start(), calls=%async_computation.2 | async-start | bytes 4325376 | tf_op jit(solution)/shard_map/all_gather | solution.py:59
  211.0 3.0 copy-start
  214.0 1.8 copy-start.3
  217.4 33.6 %copy-start.2 = (bf16[64,32,128]{2,1,0:T(8,128)(2,1)S(1)}, bf16[64,32,128]{2,1,0:T(8,128)(2,1)}, u32[]{:S(2)}) copy-start(bf16[64,32,128]{2,1,0:T(8,128)(2,1)} %param.5) | copy-start | bytes 1572868
  219.2 67.6 %all-to-all-start = ((bf16[2,4,512,128]{3,1,0,2:T(4,128)(2,1)}), bf16[2,4,512,128]{3,1,0,2:T(4,128)(2,1)S(1)}, u32[]{:S(2)}, u32[]{:S(2)}) async-start(bf16[2,4,512,128]{3,1,0,2:T(4,128)(2,1)} %copy.25), calls=%async_computation | async-start | bytes 2097152 | tf_op jit(solution)/shard_map/all_to_all | solution.py:63
  364.2 2.2 copy-start.1
Sparse Core Ops, SparseCore 0:
  9.4 201.5 all-gather.1
where the time goes:
time: 377 us
  waiting for transfers between devices  240 us (64%)
  blocking collectives  73.9 us (20%)
  starting transfers between devices  31.8 us (8%)
  between operations  13.6 us (4%)
  matrix products  8.71 us (2%)
  local copies, waits for them, and re-layouts  7.07 us (2%)
    all_gather x1, waiting for transfers between devices, on_device(): piece = lax.all_gather(right_orbitals, 'pt', axis=2, tiled=True)  204 us
    all_to_all x1, blocking collectives, on_device(): lax.all_to_all(spatial, 'kg', split_axis=1, concat_axis=2, tiled=True)  73.9 us
    all_to_all x1, waiting for transfers between devices, on_device(): lax.all_to_all(pairs, 'kg', split_axis=2, concat_axis=1, tiled=True)  35.3 us
    all_to_all x1, starting transfers between devices, on_device(): lax.all_to_all(pairs, 'kg', split_axis=2, concat_axis=1, tiled=True)  31.8 us
  transfers between devices with their start and end apart: 2, of which 2 were waited for; matrix products, arithmetic and copies ran while one was open for 0% of the time, Pallas kernels for 0%

commit v1 on v0

--- a/solution.py
+++ b/solution.py
@@ -56,7 +56,9 @@
 def on_device(left_orbitals, right_orbitals, coulomb):
     left_re = left_orbitals[0]
     left_im = left_orbitals[1]
-    piece = lax.all_gather(right_orbitals, "pt", axis=2, tiled=True)
+    piece = jnp.concatenate(
+        lax.all_to_all(jnp.stack([right_orbitals] * lax.axis_size("pt")), "pt", 0, 0), axis=2
+    )
     pair_re = cross(piece[0], left_re) + cross(piece[1], left_im)
     pair_im = cross(piece[0], left_im) - cross(piece[1], left_re)
     pairs = jnp.stack([pair_re, pair_im]).astype(jnp.bfloat16)

time: 377 us -> 523 us (1.39)
  the two profiles are of different devices: /device:TPU:39 before, /device:TPU:16 now
where the time goes in v1:
time: 523 us
  blocking collectives  240 us (46%)
  waiting for transfers between devices  239 us (46%)
  between operations  13.6 us (3%)
  starting transfers between devices  10.6 us (2%)
  matrix products  9.14 us (2%)
  local copies, waits for them, and re-layouts  8.27 us (2%)
    all_gather x1, waiting for transfers between devices, on_device(): lax.all_gather(right_orbitals, 'pt', axis=2, tiled=True)  212 us
    all_to_all x1, blocking collectives, on_device(): lax.all_to_all(jnp.stack([right_orbitals] * lax.axis_size('pt')), 'pt', 0...  198 us
    all_to_all x1, blocking collectives, on_device(): lax.all_to_all(spatial, 'kg', split_axis=1, concat_axis=2, tiled=True)  41.7 us
    all_to_all x1, waiting for transfers between devices, on_device(): lax.all_to_all(pairs, 'kg', split_axis=2, concat_axis=1, tiled=True)  26.4 us
    all_to_all x1, starting transfers between devices, on_device(): lax.all_to_all(pairs, 'kg', split_axis=2, concat_axis=1, tiled=True)  10.6 us
  transfers between devices with their start and end apart: 2, of which 2 were waited for; matrix products, arithmetic and copies ran while one was open for 1% of the time, Pallas kernels for 0%

profile of v1, /device:TPU:16, one launch (start us, length us, event | category | flops | bytes accessed | tf_op | source)
XLA Modules:
  0.0 522.5 jit_solution(6353911891964659102)
XLA Ops:
  6.5 1.4 stack.17
  8.0 198.4 %all_to_all.35 = bf16[32,2,4,16,512]{4,3,2,1,0:T(8,128)(2,1)S(1)} all-to-all(bf16[32,2,4,16,512]{4,3,2,1,0:T(8,128)(2,1)S(1)} %stack.17), channel_id=1, replica_groups=mesh['kg'=16,'pt'=32] {'pt'}, dimensions={0} | all-to-all | bytes 8388608 | tf_op jit(solution)/shard_map/all_to_all | solution.py:60
  206.4 0.8 fusion.35
  207.2 0.2 copy.25
  207.4 1.0 copy-done.1
  208.4 0.7 fusion.20
  209.1 0.7 fusion.16
  209.8 0.2 copy.26
  210.0 0.7 fusion.13
  210.7 0.7 fusion.12
  211.5 1.8 copy.27
  213.3 10.6 %all-to-all-start.1 = ((bf16[2,4,512,128]{3,1,0,2:T(4,128)(2,1)}), bf16[2,4,512,128]{3,1,0,2:T(4,128)(2,1)S(1)}, u32[]{:S(2)}, u32[]{:S(2)}) async-start(bf16[2,4,512,128]{3,1,0,2:T(4,128)(2,1)} %copy.27), calls=%async_computation.1 | async-start | bytes 2097152 | tf_op jit(solution)/shard_map/all_to_all | solution.py:65
  223.9 0.7 all-gather.2.cloned.1.call-update
  224.6 0.2 copy.24
  224.8 0.1 fusion.32
  225.0 26.4 %all-to-all-done.1 = bf16[2,4,512,128]{3,1,0,2:T(4,128)(2,1)S(1)} async-done(((bf16[2,4,512,128]{3,1,0,2:T(4,128)(2,1)}), bf16[2,4,512,128]{3,1,0,2:T(4,128)(2,1)S(1)}, u32[]{:S(2)}, u32[]{:S(2)}) %all-to-all-start.1) | async-done | bytes 1048608 | tf_op jit(solution)/shard_map/all_to_all | solution.py:65
  251.4 0.3 copy.28
  251.7 0.5 copy.52
  252.1 0.7 copy.29
  252.8 0.4 multiply_convert_fusion
  253.2 0.7 copy.30
  253.9 0.5 fusion.5
  254.5 0.2 copy.46
  254.7 0.1 copy.31
  254.9 41.7 %all_to_all.36 = bf16[2,64,32,128]{3,2,0,1:T(8,128)(2,1)S(1)} all-to-all(bf16[2,64,32,128]{3,2,0,1:T(8,128)(2,1)S(1)} %copy.31), channel_id=1, replica_groups=mesh['kg'=16,'pt'=32] {'kg'}, dimensions={1} | all-to-all | bytes 2097152 | tf_op jit(solution)/shard_map/all_to_all | solution.py:67
  296.7 0.1 fusion.36
  296.9 211.8 %all-gather.2.cloned.1.call-done = bf16[2,4,512,512]{3,2,1,0:T(8,128)(2,1)} async-done(((bf16[2,4,16,512]{3,2,1,0:T(8,128)(2,1)}), bf16[2,4,512,512]{3,2,1,0:T(8,128)(2,1)}) %all-gather.2.cloned.1.call-update) | async-done | bytes 4194320 | tf_op jit(solution)/shard_map/all_gather | solution.py:68
  508.7 2.2 fusion.2
  511.0 2.1 fusion.1
  513.1 0.5 fusion.7
  513.6 0.5 fusion.9
  514.1 1.6 pad_maximum_fusion
  (13 shorter events, 0.4 us)
Async XLA Ops:
  207.2 1.2 copy-start.1
  211.5 13.1 %copy-start.2 = (bf16[64,32,128]{2,1,0:T(8,128)(2,1)S(1)}, bf16[64,32,128]{2,1,0:T(8,128)(2,1)}, u32[]{:S(2)}) copy-start(bf16[64,32,128]{2,1,0:T(8,128)(2,1)} %param.5) | copy-start | bytes 1572868
  213.3 38.1 %all-to-all-start.1 = ((bf16[2,4,512,128]{3,1,0,2:T(4,128)(2,1)}), bf16[2,4,512,128]{3,1,0,2:T(4,128)(2,1)S(1)}, u32[]{:S(2)}, u32[]{:S(2)}) async-start(bf16[2,4,512,128]{3,1,0,2:T(4,128)(2,1)} %copy.27), calls=%async_computation.1 | async-start | bytes 2097152 | tf_op jit(solution)/shard_map/all_to_all | solution.py:65
  223.9 284.8 %all-gather.2.cloned.1.call-start = ((), (), s32[]{:S(2)}) async-start(), calls=%async_computation.3 | async-start | bytes 4325376 | tf_op jit(solution)/shard_map/all_gather | solution.py:68
  508.7 4.3 copy-start
Sparse Core Ops, SparseCore 0:
  226.8 281.8 all-gather.1
